TPU v7x, 128 devices: a whole 4x4x4 slice. The times are simulated.
128 devices in a mesh: lat: 8 (over x, z_lo), lon: 16 (over z_hi, y, core).
Axes of the slice: x: 4, y: 4, z: 4 (z_hi: 2, z_lo: 2; z = z_hi * 2 + z_lo), core: 2. Of those that a mesh axis runs over, the one named last changes fastest.
Arguments:
- tokens: bfloat16 [192, 384, 2, 512], P('lat', 'lon'), may hold values from -6 to 6
- cotangent: bfloat16 [192, 384, 2, 512], P('lat', 'lon'), may hold values from -6 to 6
- norm_gain: float32 [512], replicated, may hold values from 0.5 to 1.5
- w_qkv: bfloat16 [512, 1536], replicated, may hold values from -0.25 to 0.25
- w_out: bfloat16 [512, 512], replicated, may hold values from -0.25 to 0.25
- mlp_gain: float32 [512], replicated, may hold values from 0.5 to 1.5
- w_up: bfloat16 [512, 2048], replicated, may hold values from -0.25 to 0.25
- w_down: bfloat16 [2048, 512], replicated, may hold values from -0.125 to 0.125
Outputs:
- output: bfloat16 [192, 384, 2, 512], P('lat', 'lon')
- grad_tokens: bfloat16 [192, 384, 2, 512], P('lat', 'lon')
- grad_norm_gain: float32 [512], replicated
- grad_qkv: float32 [512, 1536], replicated
- grad_out: float32 [512, 512], replicated
- grad_mlp_gain: float32 [512], replicated
- grad_up: float32 [512, 2048], replicated
- grad_down: float32 [2048, 512], replicated
All inputs are finite; a program needn't handle non-finite values.
Results may differ from a plain program's by a relative error of at most 0.02.
Values may be sent and summed in bfloat16 or wider, within the bound.
No kernel may reach another device: no remote copies, remote signals or barrier semaphores. Data moves between devices by JAX's collectives and lax.ppermute only.
A program may use at most 192 MiB of HBM per device.

v0:
```python
import functools

import jax
import jax.numpy as jnp
from jax import lax
from jax.experimental import pallas as pl
from jax.experimental.pallas import tpu as pltpu
from jax.sharding import PartitionSpec as P

HD = 64
WLAT = 6
WLON = 12
LEV = 2
WIN = WLAT * WLON * LEV
D = 512
FF = 2048
HALF_LAT = WLAT // 2
HALF_LON = WLON // 2
EPS = 1e-05
F32 = jnp.float32
BF16 = jnp.bfloat16
PAIR = 2 * HD


def mm(a, b):
    return lax.dot_general(a, b, (((1,), (0,)), ((), ())), preferred_element_type=F32)


def mm_t(a, b):
    return lax.dot_general(a, b, (((1,), (1,)), ((), ())), preferred_element_type=F32)


def t_mm(a, b):
    return lax.dot_general(a, b, (((0,), (0,)), ((), ())), preferred_element_type=F32)


def normalised(values):
    mean = jnp.mean(values, axis=-1, keepdims=True)
    centred = values - mean
    var = jnp.mean(centred * centred, axis=-1, keepdims=True)
    scale = lax.rsqrt(var + EPS)
    return centred * scale, scale


def norm_pullback(xhat, scale, gain, grad):
    dxhat = grad * gain
    m1 = jnp.mean(dxhat, axis=-1, keepdims=True)
    m2 = jnp.mean(dxhat * xhat, axis=-1, keepdims=True)
    return scale * (dxhat - m1 - xhat * m2)


def gelu_parts(x):
    a = jnp.abs(x)
    t = 1.0 / (1.0 + (0.3275911 * 0.7071067811865476) * a)
    e = jnp.exp(-0.5 * x * x)
    poly = t * (0.127414796 + t * (-0.142248368 + t * (0.7107068705 + t * (-0.7265760135 + t * 0.5307027145))))
    tail = poly * e
    cdf = jnp.where(x >= 0.0, 1.0 - tail, tail)
    return cdf, 0.3989422804014327 * e


BANDS = 4
SIDES = 2


def strips():
    for band in range(BANDS):
        first = HALF_LAT + band * WLAT
        last = band == BANDS - 1
        across = [(0, WLAT, first, False)]
        if last:
            across = [(0, HALF_LAT, first, False), (HALF_LAT, HALF_LAT, 0, True)]
        for side in range(SIDES):
            left = HALF_LON + side * WLON
            along = [(0, WLON, left, False)]
            if side == SIDES - 1:
                along = [(0, HALF_LON, left, False), (HALF_LON, HALF_LON, 0, True)]
            for at_row, rows, row, far_row in across:
                for at_col, cols, col, far_col in along:
                    piece = 2 * far_row + far_col
                    if far_row and not far_col:
                        col -= HALF_LON
                    if far_col and not far_row:
                        row -= HALF_LAT
                    yield (
                        band, side, pl.ds(at_row, rows), pl.ds(at_col, cols),
                        piece, pl.ds(row, rows), pl.ds(col, cols),
                    )


SAVES = 6
STRIPS = len(list(strips()))


def gather_windows(which, field, rim_lon, rim_lat, corner, buffer, sems):
    copies = []
    for i, (band, side, to_rows, to_cols, piece, rows, cols) in enumerate(strips()):
        source = field if piece == 0 else (None, rim_lon, rim_lat, corner)[piece].at[which]
        copies.append(pltpu.make_async_copy(
            source.at[rows, cols], buffer.at[band, side, to_rows, to_cols], sems.at[i]))
    return copies


def scatter_windows(which, buffer, field, rim_lon, rim_lat, corner, sems):
    copies = []
    for i, (band, side, to_rows, to_cols, piece, rows, cols) in enumerate(strips()):
        target = field if piece == 0 else (None, rim_lon, rim_lat, corner)[piece].at[which]
        copies.append(pltpu.make_async_copy(
            buffer.at[band, side, to_rows, to_cols], target.at[rows, cols], sems.at[i]))
    return copies


def front_kernel(flag_ref, tok_ref, cot_ref, lon_ref, lat_ref, corner_ref, g1_ref, wqkv_hbm, wout_hbm, g2_ref,
                 x_out, n1_out, qkv_out, p_out, att_out, mid_out, cot_out, cotw_ref, n2_ref,
                 tok_buf, cot_buf, x_ref, n1_ref, qkv_ref, p_ref, att_ref, mid_ref, wqkv_ref, wout_ref,
                 sems, out_sems, w_sems):
    wqkv_copy = pltpu.make_async_copy(wqkv_hbm, wqkv_ref, w_sems.at[0])
    wout_copy = pltpu.make_async_copy(wout_hbm, wout_ref, w_sems.at[1])
    saves = []

    def save(source, target):
        copy = pltpu.make_async_copy(source, target, out_sems.at[len(saves)])
        copy.start()
        saves.append(copy)

    tok_copies = gather_windows(0, tok_ref, lon_ref, lat_ref, corner_ref, tok_buf, sems.at[0])
    cot_copies = gather_windows(1, cot_ref, lon_ref, lat_ref, corner_ref, cot_buf, sems.at[1])
    for copy in tok_copies + [wqkv_copy, wout_copy] + cot_copies:
        copy.start()
    for copy in tok_copies:
        copy.wait()
    for band in range(BANDS):
        for side in range(SIDES):
            w = band * SIDES + side
            x_ref[w * WIN:(w + 1) * WIN, :] = tok_buf[band, side].reshape(WIN, D)
    save(x_ref, x_out)
    tokens = x_ref.shape[0]
    count = tokens // WIN
    per_row = count // 4
    gain1 = g1_ref[...]
    gain2 = g2_ref[...]

    @pl.loop(0, count, unroll=2)
    def _(w):
        rows = pl.ds(pl.multiple_of(w * WIN, WIN), WIN)
        xhat, _ = normalised(x_ref[rows, :].astype(F32))
        n1_ref[rows, :] = (xhat * gain1).astype(BF16)

    wqkv_copy.wait()

    big = ROWS

    @pl.loop(0, tokens // big)
    def _(b):
        rows = pl.ds(pl.multiple_of(b * big, big), big)
        n1 = n1_ref[rows, :]
        qkv_ref[rows, 0:D] = (mm(n1, wqkv_ref[:, 0:D]).astype(BF16) * 0.125).astype(BF16)
        qkv_ref[rows, D:2 * D] = mm(n1, wqkv_ref[:, D:2 * D]).astype(BF16)
        qkv_ref[rows, 2 * D:3 * D] = mm(n1, wqkv_ref[:, 2 * D:3 * D]).astype(BF16)

    save(n1_ref, n1_out)
    save(qkv_ref, qkv_out)

    key_group = lax.broadcasted_iota(jnp.int32, (WIN, WIN), 0) >= WIN // 2
    query_group = lax.broadcasted_iota(jnp.int32, (WIN, WIN), 1) >= WIN // 2
    split = key_group != query_group
    low = lax.broadcasted_iota(jnp.int32, (WIN, PAIR), 1) < HD

    @pl.loop(0, count, unroll=4)
    def _(w):
        rows = pl.ds(pl.multiple_of(w * WIN, WIN), WIN)
        cut = jnp.logical_and(flag_ref[0] == 1, w >= count - per_row)
        masked = jnp.logical_and(split, cut)
        for pair in range(D // PAIR):
            lanes = slice(pair * PAIR, (pair + 1) * PAIR)
            q = qkv_ref[rows, pair * PAIR:(pair + 1) * PAIR]
            k = qkv_ref[rows, D + pair * PAIR:D + (pair + 1) * PAIR]
            v = qkv_ref[rows, 2 * D + pair * PAIR:2 * D + (pair + 1) * PAIR]
            outs = []
            for h in range(2):
                mine = low if h == 0 else jnp.logical_not(low)
                kh = jnp.where(mine, k, jnp.zeros_like(k))
                s = mm_t(kh, q)
                s = jnp.where(masked, -1000000000.0, s)
                e = jnp.exp(s - jnp.max(s, axis=0, keepdims=True))
                p = (e * (1.0 / jnp.sum(e, axis=0, keepdims=True))).astype(BF16)
                p_ref[w, 2 * pair + h] = p
                outs.append(t_mm(p, v))
            att_ref[rows, lanes] = jnp.where(low, outs[0], outs[1]).astype(BF16)
        pltpu.make_async_copy(p_ref.at[w], p_out.at[w], out_sems.at[SAVES + w]).start()

    save(att_ref, att_out)
    wout_copy.wait()

    @pl.loop(0, tokens // big)
    def _(b):
        rows = pl.ds(pl.multiple_of(b * big, big), big)
        mid = (x_ref[rows, :].astype(F32) + mm(att_ref[rows, :], wout_ref[...])).astype(BF16)
        mid_ref[rows, :] = mid
        xhat, _ = normalised(mid.astype(F32))
        n2_ref[rows, :] = (xhat * gain2).astype(BF16)

    save(mid_ref, mid_out)
    for copy in cot_copies:
        copy.wait()
    for band in range(BANDS):
        for side in range(SIDES):
            w = band * SIDES + side
            cotw_ref[w * WIN:(w + 1) * WIN, :] = cot_buf[band, side].reshape(WIN, D)
    save(cotw_ref, cot_out)
    for copy in saves:
        copy.wait()
    for w in range(count):
        pltpu.make_async_copy(p_ref.at[w], p_out.at[w], out_sems.at[SAVES + w]).wait()


CHUNK = 512
ROWS = 4 * WIN


def mlp_chunk(chunk, n2_ref, cot_ref, wup_ref, wdown_ref, down_in, dn2_in, down_out, dn2_out, hid_ref, du_ref):
    at = pl.ds(pl.multiple_of(chunk * CHUNK, CHUNK), CHUNK)

    @pl.loop(0, n2_ref.shape[0] // ROWS)
    def _(b):
        rows = pl.ds(pl.multiple_of(b * ROWS, ROWS), ROWS)
        up = mm(n2_ref[rows, :], wup_ref[:, at])
        cdf, pdf = gelu_parts(up)
        hid = (up * cdf).astype(BF16)
        hid_ref[rows, :] = hid
        dhid = mm_t(cot_ref[rows, :], wdown_ref[at, :]).astype(BF16).astype(F32)
        du = (dhid * (cdf + up * pdf)).astype(BF16)
        du_ref[rows, :] = du
        down = mm(hid, wdown_ref[at, :])
        dn2 = mm_t(du, wup_ref[:, at])
        if down_in is None:
            down_out[rows, :] = down
            dn2_out[rows, :] = dn2
        else:
            down_out[rows, :] = down_in[rows, :] + down
            dn2_out[rows, :] = dn2_in[rows, :] + dn2

    return t_mm(n2_ref[...], du_ref[...]).astype(BF16), t_mm(hid_ref[...], cot_ref[...]).astype(BF16)


def send_kernel(me_ref, n2_ref, cot_ref, wup_ref, wdown_ref, down_ref, dn2_ref, grads_ref, hid_ref, du_ref):
    for i in range(2):
        carried = (down_ref, dn2_ref) if i else (None, None)
        grads = mlp_chunk((1 - me_ref[0]) * 2 + i, n2_ref, cot_ref, wup_ref, wdown_ref,
                          *carried, down_ref, dn2_ref, hid_ref, du_ref)
        for part, grad in enumerate(grads):
            grads_ref[(2 * part + i) * CHUNK:(2 * part + i + 1) * CHUNK, :] = grad


def keep_first_kernel(me_ref, n2_ref, cot_ref, wup_ref, wdown_ref, down_in, dn2_in,
                      down_ref, dn2_ref, early_ref, hid_ref, du_ref):
    grads = mlp_chunk(me_ref[0] * 2, n2_ref, cot_ref, wup_ref, wdown_ref,
                      down_in, dn2_in, down_ref, dn2_ref, hid_ref, du_ref)
    for part, grad in enumerate(grads):
        early_ref[part * CHUNK:(part + 1) * CHUNK, :] = grad


def keep_second_kernel(me_ref, n2_ref, cot_ref, wup_ref, wdown_ref, down_in, dn2_in, early_ref, got_ref,
                       down_hbm, dn2_hbm, grads_ref, hid_ref, du_ref, down_ref, dn2_ref, sems):
    grads = mlp_chunk(me_ref[0] * 2 + 1, n2_ref, cot_ref, wup_ref, wdown_ref,
                      down_in, dn2_in, down_ref, dn2_ref, hid_ref, du_ref)
    copies = [
        pltpu.make_async_copy(down_ref, down_hbm, sems.at[0]),
        pltpu.make_async_copy(dn2_ref, dn2_hbm, sems.at[1]),
    ]
    for copy in copies:
        copy.start()
    for part, grad in enumerate(grads):
        for i in range(2):
            rows = slice((2 * part + i) * CHUNK, (2 * part + i + 1) * CHUNK)
            mine = grad if i else early_ref[part * CHUNK:(part + 1) * CHUNK, :]
            grads_ref[rows, :] = (mine.astype(F32) + got_ref[rows, :].astype(F32)).astype(BF16)
    for copy in copies:
        copy.wait()


HALF = D // 2
CHIPS_N = 64
GRADS = 64
GAINS = 8


def att_grads(half, n1_ref, dqkv_ref, att_ref, dmid_ref, out_ref):
    per = D // (CHIPS_N // 4)
    lanes = pl.ds(pl.multiple_of(half * HALF, HALF), HALF)
    for part in range(4):
        if part < 3:
            part_lanes = pl.ds(pl.multiple_of(part * D + half * HALF, HALF), HALF)
            grad = t_mm(n1_ref[...], dqkv_ref[:, part_lanes])
        else:
            grad = t_mm(att_ref[...], dmid_ref[:, lanes])
        grad = grad.astype(BF16)
        first = part * (CHIPS_N // 4)
        for block in range(2):
            piece = grad[:, block * 128:(block + 1) * 128].reshape(CHIPS_N // 4, per, 128)
            out_ref[first:first + CHIPS_N // 4, block * per:(block + 1) * per, :] = piece


def att_back(first, last, datt_ref, qkv_ref, p_ref, dqkv_ref):
    low = lax.broadcasted_iota(jnp.int32, (WIN, PAIR), 1) < HD

    @pl.loop(first, last, unroll=4)
    def _(w):
        rows = pl.ds(pl.multiple_of(w * WIN, WIN), WIN)
        for pair in range(D // PAIR):
            lanes = slice(pair * PAIR, (pair + 1) * PAIR)
            q = qkv_ref[rows, pair * PAIR:(pair + 1) * PAIR]
            k = qkv_ref[rows, D + pair * PAIR:D + (pair + 1) * PAIR]
            v = qkv_ref[rows, 2 * D + pair * PAIR:2 * D + (pair + 1) * PAIR]
            da = datt_ref[rows, lanes]
            dqs, dks, dvs = [], [], []
            for h in range(2):
                mine = low if h == 0 else jnp.logical_not(low)
                vh = jnp.where(mine, v, jnp.zeros_like(v))
                p = p_ref[w, 2 * pair + h]
                pf = p.astype(F32)
                dp = mm_t(vh, da).astype(BF16).astype(F32)
                ds = (pf * (dp - jnp.sum(dp * pf, axis=0, keepdims=True))).astype(BF16)
                dvs.append(mm(p, da))
                dks.append(mm(ds, q))
                dqs.append(t_mm(ds, k))
            dqkv_ref[rows, pair * PAIR:(pair + 1) * PAIR] = (jnp.where(low, dqs[0], dqs[1]) * 0.125).astype(BF16)
            dqkv_ref[rows, D + pair * PAIR:D + (pair + 1) * PAIR] = jnp.where(low, dks[0], dks[1]).astype(BF16)
            dqkv_ref[rows, 2 * D + pair * PAIR:2 * D + (pair + 1) * PAIR] = jnp.where(low, dvs[0], dvs[1]).astype(BF16)


def start_loads(pairs, sems):
    loads = []
    for i, (source, target) in enumerate(pairs):
        loads.append(pltpu.make_async_copy(source, target, sems.at[i]))
        loads[-1].start()
    return loads


def back_kernel(cot_hbm, mid_hbm, down_hbm, dn2_hbm, wout_hbm, qkv_hbm, p_hbm, att_hbm, n1_hbm, g2_ref,
                res_out, dmid_out, dqkv_out, dg2_ref, att_ref, n1_ref, dmid_ref, dqkv_ref,
                cot_ref, mid_ref, down_ref, dn2_ref, wout_ref, qkv_ref, p_ref, datt_ref, res_ref, in_sems, sems):
    loads = start_loads((
        (cot_hbm, cot_ref), (mid_hbm, mid_ref), (down_hbm, down_ref), (dn2_hbm, dn2_ref),
        (wout_hbm, wout_ref), (qkv_hbm, qkv_ref), (p_hbm, p_ref), (att_hbm, att_ref), (n1_hbm, n1_ref),
    ), in_sems)
    gain2 = g2_ref[...]
    dg2_ref[...] = jnp.zeros_like(dg2_ref)
    tokens = cot_ref.shape[0]
    for load in loads[:4]:
        load.wait()

    @pl.loop(0, tokens // WIN, unroll=2)
    def _(b):
        rows = pl.ds(pl.multiple_of(b * WIN, WIN), WIN)
        mid = mid_ref[rows, :].astype(F32)
        res_ref[rows, :] = (mid + down_ref[rows, :]).astype(BF16)
        xhat, scale = normalised(mid)
        dn2 = dn2_ref[rows, :].astype(BF16).astype(F32)
        dg2_ref[...] += jnp.sum(dn2 * xhat, axis=0, keepdims=True)
        dmid = cot_ref[rows, :].astype(F32) + norm_pullback(xhat, scale, gain2, dn2)
        dmid_ref[rows, :] = dmid.astype(BF16)

    saves = [
        pltpu.make_async_copy(res_ref, res_out, sems.at[0]),
        pltpu.make_async_copy(dmid_ref, dmid_out, sems.at[1]),
    ]
    for copy in saves:
        copy.start()
    loads[4].wait()

    @pl.loop(0, tokens // ROWS)
    def _(b):
        rows = pl.ds(pl.multiple_of(b * ROWS, ROWS), ROWS)
        datt_ref[rows, :] = mm_t(dmid_ref[rows, :], wout_ref[...]).astype(BF16)

    loads[5].wait()
    loads[6].wait()
    att_back(0, tokens // WIN, datt_ref, qkv_ref, p_ref, dqkv_ref)
    saves.append(pltpu.make_async_copy(dqkv_ref, dqkv_out, sems.at[2]))
    saves[-1].start()
    for copy in loads[7:] + saves:
        copy.wait()


def tokens_kernel(dqkv_hbm, wqkv_hbm, x_hbm, dmid_hbm, res_hbm, g1_ref, after_ref,
                  out_ref, grad_ref, lon_ref, lat_ref, corner_ref, dg1_ref,
                  dqkv_ref, wqkv_ref, x_ref, dmid_ref, res_ref, dx_ref, res_buf, dx_buf, in_sems, sems):
    loads = start_loads((
        (res_hbm, res_ref), (dqkv_hbm, dqkv_ref), (wqkv_hbm, wqkv_ref), (x_hbm, x_ref), (dmid_hbm, dmid_ref),
    ), in_sems)
    gain1 = g1_ref[...]
    tokens = x_ref.shape[0]
    dg1_ref[...] = jnp.zeros_like(dg1_ref)
    loads[0].wait()
    for band in range(BANDS):
        for side in range(SIDES):
            w = band * SIDES + side
            res_buf[band, side] = res_ref[w * WIN:(w + 1) * WIN, :].reshape(WLAT, WLON, LEV, D)
    res_copies = scatter_windows(0, res_buf, out_ref, lon_ref, lat_ref, corner_ref, sems.at[0])
    for copy in res_copies:
        copy.start()
    for load in loads[1:]:
        load.wait()

    @pl.loop(0, tokens // ROWS)
    def _(b):
        rows = pl.ds(pl.multiple_of(b * ROWS, ROWS), ROWS)
        dn1 = mm_t(dqkv_ref[rows, :], wqkv_ref[...]).astype(BF16).astype(F32)
        xhat, scale = normalised(x_ref[rows, :].astype(F32))
        dg1_ref[...] += jnp.sum(dn1 * xhat, axis=0, keepdims=True)
        dx = dmid_ref[rows, :].astype(F32) + norm_pullback(xhat, scale, gain1, dn1)
        dx_ref[rows, :] = dx.astype(BF16)

    for band in range(BANDS):
        for side in range(SIDES):
            w = band * SIDES + side
            dx_buf[band, side] = dx_ref[w * WIN:(w + 1) * WIN, :].reshape(WLAT, WLON, LEV, D)
    dx_copies = scatter_windows(1, dx_buf, grad_ref, lon_ref, lat_ref, corner_ref, sems.at[1])
    for copy in dx_copies:
        copy.start()
    for copy in res_copies + dx_copies:
        copy.wait()


SHARE = FF // CHIPS_N
MLP = SHARE * D // 128
ALL = GRADS + GAINS + MLP


def total_of(parts_ref, rows):
    total = parts_ref[0, rows, :].astype(F32)
    for chip in range(1, CHIPS_N):
        total += parts_ref[chip, rows, :].astype(F32)
    return total.astype(BF16)


def half_kernel(half_ref, n1_ref, dqkv_ref, att_ref, dmid_ref, out_ref):
    att_grads(half_ref[0], n1_ref, dqkv_ref, att_ref, dmid_ref, out_ref)


def add_kernel(keep_ref, got_ref, out_ref):
    for chip in range(CHIPS_N):
        out_ref[chip] = (keep_ref[chip].astype(F32) + got_ref[chip].astype(F32)).astype(BF16)


def share_mlp_kernel(sums_ref, after_ref, tile_ref):
    del after_ref
    total = total_of(sums_ref, slice(0, SHARE))
    for block in range(D // 128):
        tile_ref[block * SHARE:(block + 1) * SHARE, :] = total[:, block * 128:(block + 1) * 128]


def share_kernel(parts_ref, tile_ref, dg1_ref, dg2_ref, out_ref, share_ref, sems):
    share_ref[GRADS + GAINS:, :] = tile_ref[...]
    share_ref[GRADS:GRADS + GAINS, :] = jnp.concatenate(
        [ref[:, block * 128:(block + 1) * 128] for ref in (dg1_ref, dg2_ref) for block in range(D // 128)]).astype(BF16)
    share_ref[0:GRADS, :] = total_of(parts_ref, slice(0, GRADS))
    copies = [pltpu.make_async_copy(share_ref, out_ref.at[chip], sems.at[chip]) for chip in range(CHIPS_N)]
    for copy in copies:
        copy.start()
    for copy in copies:
        copy.wait()


def unpack_kernel(mine, half_ref, all_ref, gains_in, *refs):
    (gup_hbm, gdown_hbm, gqkv_hbm, gout_hbm, gains_ref, gup_ref, gdown_ref, att_ref, sems) = refs if mine else refs[4:]
    half = half_ref[0]
    wide = FF // 2
    copies = []

    def send(source, target):
        copies.append(pltpu.make_async_copy(source, target, sems.at[len(copies)]))
        copies[-1].start()

    blocks = [(slice(GRADS + GAINS + i * SHARE, GRADS + GAINS + (i + 1) * SHARE), i * 128) for i in range(D // 128)]
    quarter = CHIPS_N // 4
    for rows, lane in blocks:
        gdown_ref[:, lane:lane + 128] = all_ref[2 * quarter:, rows, :].reshape(wide, 128).astype(F32)
    send(gdown_ref, gdown_hbm.at[pl.ds(pl.multiple_of(half * wide, wide), wide), :])
    for j in range(2):
        for rows, lane in blocks:
            piece = all_ref[j * quarter:(j + 1) * quarter, rows, :].reshape(D, 128)
            gup_ref[:, j * D + lane:j * D + lane + 128] = piece.astype(F32)
    send(gup_ref, gup_hbm.at[:, pl.ds(pl.multiple_of(half * wide, wide), wide)])
    per = GRADS // 2
    for part in range(4):
        for block in range(2):
            piece = all_ref[part * quarter:(part + 1) * quarter, block * per:(block + 1) * per, :].reshape(D, 128)
            att_ref[part, :, block * 128:(block + 1) * 128] = piece.astype(F32)
        out, first = (gqkv_hbm, part * D) if part < 3 else (gout_hbm, 0)
        send(att_ref.at[part], out.at[:, pl.ds(pl.multiple_of(half * HALF + first, HALF), HALF)])
    gains = all_ref[0, GRADS:GRADS + GAINS, :].astype(F32)
    for chip in range(1, CHIPS_N):
        gains += all_ref[chip, GRADS:GRADS + GAINS, :].astype(F32)
    gains_ref[...] = gains if mine else gains_in[...] + gains
    for copy in copies:
        copy.wait()


def pack_kernel(tok_ref, cot_ref, lon_ref, lat_ref, corner_ref, sems):
    copies = []
    for which, ref in enumerate((tok_ref, cot_ref)):
        below, right = pl.ds(HALF_LAT, ref.shape[0] - HALF_LAT), pl.ds(HALF_LON, ref.shape[1] - HALF_LON)
        top, left = pl.ds(0, HALF_LAT), pl.ds(0, HALF_LON)
        for i, (rows, cols, out) in enumerate(((below, left, lon_ref), (top, right, lat_ref), (top, left, corner_ref))):
            copies.append(pltpu.make_async_copy(ref.at[rows, cols], out.at[which], sems.at[which, i]))
    for copy in copies:
        copy.start()
    for copy in copies:
        copy.wait()


def place_kernel(out_in, grad_in, lon_ref, lat_ref, corner_ref, after_ref, out_ref, grad_ref, sems):
    del out_in, grad_in, after_ref
    copies = []
    for which, ref in enumerate((out_ref, grad_ref)):
        below, right = pl.ds(HALF_LAT, ref.shape[0] - HALF_LAT), pl.ds(HALF_LON, ref.shape[1] - HALF_LON)
        top, left = pl.ds(0, HALF_LAT), pl.ds(0, HALF_LON)
        for i, (rows, cols, rim) in enumerate(((below, left, lon_ref), (top, right, lat_ref), (top, left, corner_ref))):
            copies.append(pltpu.make_async_copy(rim.at[which], ref.at[rows, cols], sems.at[which, i]))
    for copy in copies:
        copy.start()
    for copy in copies:
        copy.wait()


def params(mib=32):
    return pltpu.CompilerParams(vmem_limit_bytes=mib * 2**20)


def cost(flops, moved):
    return pl.CostEstimate(flops=flops, bytes_accessed=moved, transcendentals=0)


def shape(dims, dtype=BF16):
    return jax.ShapeDtypeStruct(dims, dtype)


SM = pl.BlockSpec(memory_space=pltpu.SMEM)
VM = pl.BlockSpec(memory_space=pltpu.VMEM)


ANY = pl.BlockSpec(memory_space=pl.ANY)
HB = pl.BlockSpec(memory_space=pltpu.HBM)


def rim_shapes(rows, cols, levels):
    return [
        shape((2, rows - HALF_LAT, HALF_LON, levels, D)),
        shape((2, HALF_LAT, cols - HALF_LON, levels, D)),
        shape((2, HALF_LAT, HALF_LON, levels, D)),
    ]


def pack(tokens, cotangent):
    return pl.pallas_call(
        pack_kernel,
        name="pack",
        in_specs=[ANY] * 2,
        out_specs=[VM] * 3,
        out_shape=[local(rim.shape) for rim in rim_shapes(*tokens.shape[:3])],
        scratch_shapes=[pltpu.SemaphoreType.DMA((2, 3))],
    )(tokens, cotangent)


def place(output, grad, lon, lat, corner, after):
    return pl.pallas_call(
        place_kernel,
        name="place",
        in_specs=[ANY] * 2 + [VM] * 3 + [ANY],
        out_specs=[ANY] * 2,
        out_shape=[shape(output.shape), shape(grad.shape)],
        input_output_aliases={0: 0, 1: 1},
        scratch_shapes=[pltpu.SemaphoreType.DMA((2, 3))],
        cost_estimate=cost(10**9, 2**21),
    )(output, grad, lon, lat, corner, after)


WINDOWED = (BANDS, SIDES, WLAT, WLON, LEV, D)


def local(dims, dtype=BF16):
    return pltpu.VMEM(dims, dtype)


def held(*arrays):
    return [pltpu.with_memory_space_constraint(array, pltpu.VMEM) for array in arrays]


def far(*arrays):
    return [pltpu.with_memory_space_constraint(array, pltpu.HBM) for array in arrays]


def front(flag, tok, cot, lon, lat, corner, g1, wqkv, wout, g2):
    tokens = tok.size // D
    count = tokens // WIN
    saved = [(tokens, D), (tokens, D), (tokens, 3 * D), (count, D // HD, WIN, WIN), (tokens, D), (tokens, D)]
    return pl.pallas_call(
        front_kernel,
        name="front",
        in_specs=[SM] + [ANY] * 5 + [VM, HB, HB, VM],
        out_specs=[HB] * 7 + [VM] * 2,
        out_shape=[pltpu.HBM(dims, BF16) for dims in saved + [(tokens, D)]] + [local((tokens, D)), local((tokens, D))],
        scratch_shapes=[
            pltpu.VMEM(WINDOWED, BF16),
            pltpu.VMEM(WINDOWED, BF16),
        ] + [pltpu.VMEM(dims, BF16) for dims in saved] + [
            pltpu.VMEM((D, 3 * D), BF16),
            pltpu.VMEM((D, D), BF16),
            pltpu.SemaphoreType.DMA((2, STRIPS)),
            pltpu.SemaphoreType.DMA((SAVES + count,)),
            pltpu.SemaphoreType.DMA((2,)),
        ],
        compiler_params=params(),
        cost_estimate=cost(15 * 10**9, 10 * 2**20),
    )(flag, tok, cot, lon, lat, corner, g1, *far(wqkv, wout), g2)


def mlp(kind, me, n2, cot, wup, wdown, *carried):
    tokens = n2.shape[0]
    sums = [local((tokens, D), F32)] * 2
    scratch = [pltpu.VMEM((tokens, CHUNK), BF16)] * 2
    out_specs, aliases = [VM] * 3, {}
    if kind == "send":
        kernel, out_shape = send_kernel, sums + [shape((FF, D))]
    elif kind == "first":
        kernel, out_shape = keep_first_kernel, sums + [local((2 * CHUNK, D))]
        aliases = {5: 0, 6: 1}
    else:
        kernel, out_shape = keep_second_kernel, [pltpu.HBM((tokens, D), F32)] * 2 + [pltpu.HBM((FF, D), BF16)]
        out_specs = [HB, HB, VM]
        scratch = scratch + [pltpu.VMEM((tokens, D), F32)] * 2 + [pltpu.SemaphoreType.DMA((2,))]
    return pl.pallas_call(
        kernel,
        name="mlp_" + kind,
        in_specs=[SM, VM, VM, VM, VM] + [VM] * len(carried),
        out_specs=out_specs,
        out_shape=out_shape,
        scratch_shapes=scratch,
        input_output_aliases=aliases,
        compiler_params=params(),
        cost_estimate=cost((16 if kind == "send" else 8) * 10**9, 10 * 2**20),
    )(me, *held(n2, cot, wup, wdown, *carried))


def back(cot, mid, down, dn2, wout, qkv, p, att, n1, g2):
    tokens = cot.shape[0]
    count = tokens // WIN
    halves = pltpu.VMEM((tokens, D), BF16)
    full = pltpu.VMEM((tokens, D), F32)
    return pl.pallas_call(
        back_kernel,
        name="back",
        in_specs=[HB] * 9 + [VM],
        out_specs=[HB] * 3 + [VM] * 5,
        out_shape=[
            pltpu.HBM((tokens, D), BF16),
            pltpu.HBM((tokens, D), BF16),
            pltpu.HBM((tokens, 3 * D), BF16),
            shape((1, D), F32),
            local((tokens, D)),
            local((tokens, D)),
            local((tokens, D)),
            local((tokens, 3 * D)),
        ],
        scratch_shapes=[
            halves,
            halves,
            full,
            full,
            pltpu.VMEM((D, D), BF16),
            pltpu.VMEM((tokens, 3 * D), BF16),
            pltpu.VMEM((count, D // HD, WIN, WIN), BF16),
            halves,
            halves,
            pltpu.SemaphoreType.DMA((9,)),
            pltpu.SemaphoreType.DMA((3,)),
        ],
        compiler_params=params(40),
        cost_estimate=cost(25 * 10**9, 10 * 2**20),
    )(*far(cot, mid, down, dn2, wout, qkv, p, att, n1), g2)


def token_grads(dqkv, wqkv, x, dmid, res, g1, after, field):
    tokens = x.shape[0]
    halves = pltpu.VMEM((tokens, D), BF16)
    return pl.pallas_call(
        tokens_kernel,
        name="tokens",
        in_specs=[HB] * 5 + [VM, ANY],
        out_specs=[ANY] * 5 + [VM],
        out_shape=[shape(field), shape(field)] + rim_shapes(*field[:3]) + [shape((1, D), F32)],
        scratch_shapes=[
            pltpu.VMEM((tokens, 3 * D), BF16),
            pltpu.VMEM((D, 3 * D), BF16),
            halves,
            halves,
            halves,
            halves,
            pltpu.VMEM(WINDOWED, BF16),
            pltpu.VMEM(WINDOWED, BF16),
            pltpu.SemaphoreType.DMA((5,)),
            pltpu.SemaphoreType.DMA((2, STRIPS)),
        ],
        compiler_params=params(),
        cost_estimate=cost(6 * 10**9, 10 * 2**20),
    )(*far(dqkv, wqkv, x, dmid, res), g1, after)


def half_grads(name, half, n1, dqkv, att, dmid):
    return pl.pallas_call(
        half_kernel,
        name=name,
        in_specs=[SM] + [VM] * 4,
        out_specs=VM,
        out_shape=local((CHIPS_N, GRADS, 128)),
        compiler_params=params(),
        cost_estimate=cost(4 * 10**9, 4 * 2**20),
    )(half, *held(n1, dqkv, att, dmid))


def simple(kernel, name, out_shape, *operands, specs=None, scratch=(), mib=56):
    return pl.pallas_call(
        kernel,
        name=name,
        in_specs=specs or [VM] * len(operands),
        out_specs=VM if not scratch else HB,
        out_shape=out_shape,
        scratch_shapes=scratch,
        compiler_params=params(mib),
        cost_estimate=cost(10**9, 4 * 2**20),
    )(*operands)


def unpack(half, gathered, carried=None):
    mine = carried is None
    outs = [pltpu.HBM((D, FF), F32), pltpu.HBM((FF, D), F32), pltpu.HBM((D, 3 * D), F32), pltpu.HBM((D, D), F32)]
    gains = jnp.zeros((GAINS, 128), F32) if mine else carried[4]
    return pl.pallas_call(
        functools.partial(unpack_kernel, mine),
        name="unpack_mine" if mine else "unpack_theirs",
        in_specs=[SM, VM, VM] + ([] if mine else [HB] * 4),
        out_specs=[HB] * 4 + [VM],
        out_shape=outs + [shape((GAINS, 128), F32)],
        scratch_shapes=[
            pltpu.VMEM((D, FF // 2), F32),
            pltpu.VMEM((FF // 2, D), F32),
            pltpu.VMEM((4, D, HALF), F32),
            pltpu.SemaphoreType.DMA((6,)),
        ],
        input_output_aliases={} if mine else {3: 0, 4: 1, 5: 2, 6: 3},
        compiler_params=params(40),
        cost_estimate=cost(10**9, 10 * 2**20),
    )(half, gathered, gains, *([] if mine else far(*carried[:4])))


LAT = ("x", "zl")
LON = ("zh", "y", "c")
CHIPS = ("y", "x", "zh", "zl")


def send_rims(lon, lat, corner, distance):
    lats, lons = lax.axis_size(LAT), lax.axis_size(LON)
    moved = []
    for block, down, across in ((lon, 0, distance), (lat, distance, 0), (corner, distance, distance)):
        route = [
            (i * lons + j, (i + down) % lats * lons + (j + across) % lons)
            for i in range(lats) for j in range(lons)
        ]
        moved.append(lax.ppermute(block, LAT + LON, route))
    return moved


def other_core(block):
    return lax.ppermute(block, "c", [(0, 1), (1, 0)])


def exchange(parts):
    return lax.all_to_all(parts, CHIPS, 0, 0, tiled=True)


def shards(tokens, cotangent, norm_gain, w_qkv, w_out, mlp_gain, w_up, w_down):
    g1 = norm_gain.reshape(1, D)
    g2 = mlp_gain.reshape(1, D)
    last_band = lax.axis_index(LAT) == lax.axis_size(LAT) - 1
    flag = last_band.astype(jnp.int32).reshape(1)
    me = lax.axis_index("c").astype(jnp.int32).reshape(1)

    rims = send_rims(*pack(tokens, cotangent), -1)
    x, n1, qkv, p, att, mid, cot_far, cot, n2 = front(flag, tokens, cotangent, *rims, g1, w_qkv, w_out, g2)
    fixed = (me, n2, cot, w_up, w_down)
    down, dn2, grads = mlp("send", *fixed)
    got = other_core(grads)
    down, dn2, early = mlp("first", *fixed, down, dn2)
    down, dn2, grads = mlp("second", *fixed, down, dn2, early, got)
    sums = exchange(grads.reshape(CHIPS_N, SHARE, D))
    res, dmid_far, dqkv_far, dg2, att, n1, dmid, dqkv = back(cot_far, mid, down, dn2, w_out, qkv, p, att, n1, g2)
    got = other_core(half_grads("send", 1 - me, n1, dqkv, att, dmid))
    keep = half_grads("keep", me, n1, dqkv, att, dmid)
    added = simple(add_kernel, "add", pltpu.HBM((CHIPS_N, GRADS, 128), BF16), *held(keep, got), mib=32)
    att_sums = exchange(added)
    tile = simple(share_mlp_kernel, "share_mlp", shape((MLP, 128)), sums, added, specs=[VM, ANY])
    output, grad_tokens, lon, lat, corner, dg1 = token_grads(
        dqkv_far, w_qkv, x, dmid_far, res, g1, added, tokens.shape)
    att_sums, tile, dg1 = lax.optimization_barrier((att_sums, tile, dg1))
    rims = send_rims(lon, lat, corner, 1)
    shares = simple(
        share_kernel, "share", pltpu.HBM((CHIPS_N, ALL, 128), BF16), *held(att_sums), tile, dg1, dg2, mib=32,
        scratch=[pltpu.VMEM((ALL, 128), BF16), pltpu.SemaphoreType.DMA((CHIPS_N,))])
    gathered = exchange(shares)
    theirs = other_core(gathered)
    grads = unpack(1 - me, theirs, unpack(me, gathered))
    output, grad_tokens = place(output, grad_tokens, *rims, grads[4])
    gup, gdown, gqkv, gout, gains = grads
    gains = gains.reshape(2, D)
    return (output, grad_tokens, gains[0], gqkv, gout, gains[1], gup, gdown)


def solution(mesh):
    field = P(LAT, LON, None, None)
    mesh = jax.sharding.Mesh(mesh.devices.reshape(4, 2, 2, 4, 2), ("x", "zl", "zh", "y", "c"))
    return jax.shard_map(
        shards,
        mesh=mesh,
        in_specs=(field, field, P(), P(), P(), P(), P(), P()),
        out_specs=(field, field, P(), P(), P(), P(), P(), P()),
        check_vma=False,
    )
```

profile of v0, /device:TPU:1, one launch (start us, length us, event | category | flops | bytes accessed | tf_op | source)
XLA Modules:
  0.0 192.8 jit_solution(4511080164303891515)
XLA Ops:
  4.3 3.9 %collective-permute-start.1 = (bf16[2,3,18,2,512]{4,3,2,1,0:T(2,128)(2,1)S(1)}, bf16[2,3,18,2,512]{4,3,2,1,0:T(2,128)(2,1)S(1)}, u32[]{:S(2)}, u32[]{:S(2)}) collective-permute-start(bf16[2,3,18,2,512]{4,3,2,1,0:T(2,128)(2,1)S(1)} %get-tuple-element.59), channel_id=1, source_target_pairs={{0,112},{1,113},{2,114},{3,115},{4,116},{5,117},{6,118},{7,119},{8... | collective-permute-start | bytes 663560 | tf_op jit(solution)/shard_map/ppermute | solution.py:771
  8.2 5.8 %collective-permute-start.2 = (bf16[2,3,6,2,512]{4,3,2,1,0:T(2,128)(2,1)S(1)}, bf16[2,3,6,2,512]{4,3,2,1,0:T(2,128)(2,1)S(1)}, u32[]{:S(2)}, u32[]{:S(2)}) collective-permute-start(bf16[2,3,6,2,512]{4,3,2,1,0:T(2,128)(2,1)S(1)} %get-tuple-element.60), channel_id=1, source_target_pairs={{0,127},{1,112},{2,113},{3,114},{4,115},{5,116},{6,117},{7,118},{8... | collective-permute-start | bytes 221192 | tf_op jit(solution)/shard_map/ppermute | solution.py:771
  14.0 2.0 %collective-permute-done.2.corner_ref = bf16[2,3,6,2,512]{4,3,2,1,0:T(2,128)(2,1)S(1)} collective-permute-done((bf16[2,3,6,2,512]{4,3,2,1,0:T(2,128)(2,1)S(1)}, bf16[2,3,6,2,512]{4,3,2,1,0:T(2,128)(2,1)S(1)}, u32[]{:S(2)}, u32[]{:S(2)}) %collective-permute-start.2) | collective-permute-done | bytes 73760 | tf_op jit(solution)/shard_map/ppermute | solution.py:771
  16.1 12.7 %front.1 = (bf16[1152,512]{1,0:T(8,128)(2,1)}, bf16[1152,512]{1,0:T(8,128)(2,1)}, bf16[1152,1536]{1,0:T(8,128)(2,1)}, bf16[8,8,144,144]{3,2,1,0:T(8,128)(2,1)}, ...) custom-call(s32[1]{0:T(128)} %bitcast.flag_ref, ...), custom_call_target="tpu_custom_call" | custom-call | flops 15000000512 | bytes 10485760 | tf_op jit(solution)/shard_map/front/pallas_call | solution.py:599
  28.8 10.7 %mlp_send.1 = (f32[1152,512]{1,0:T(8,128)S(1)}, f32[1152,512]{1,0:T(8,128)S(1)}, bf16[2048,512]{1,0:T(8,128)(2,1)S(1)}) custom-call(s32[1]{0:T(128)} %bitcast.3.me_ref.half_ref, bf16[1152,512]{1,0:T(8,128)(2,1)S(1)} %get-tuple-element.63.n2_ref, bf16[1152,512]{1,0:T(8,128)(2,1)S(1)} %get-tuple-element.64.cot_ref, bf16[512,2048]{1,0:T(8,128)(2,1)S(1)} %copy-done.5, ...), custom_call_target="tpu_custom_call" | custom-call | flops 16000000000 | bytes 10485760 | tf_op jit(solution)/shard_map/mlp_send/pallas_call | solution.py:634
  39.5 3.6 %collective-permute-start.3 = (bf16[2048,512]{1,0:T(8,128)(2,1)S(1)}, bf16[2048,512]{1,0:T(8,128)(2,1)S(1)}, u32[]{:S(2)}, u32[]{:S(2)}) collective-permute-start(bf16[2048,512]{1,0:T(8,128)(2,1)S(1)} %get-tuple-element.70), channel_id=1, source_target_pairs={{0,1},{1,0},{2,3},{3,2},{4,5},{5,4},{6,7},{7,6},{8,9},{9,8},{10,11... | collective-permute-start | bytes 6291464 | tf_op jit(solution)/shard_map/ppermute | solution.py:776
  43.1 5.8 %mlp_first.1 = (f32[1152,512]{1,0:T(8,128)S(1)}, f32[1152,512]{1,0:T(8,128)S(1)}, bf16[1024,512]{1,0:T(8,128)(2,1)S(1)}) custom-call(s32[1]{0:T(128)} %bitcast.3.me_ref.half_ref, bf16[1152,512]{1,0:T(8,128)(2,1)S(1)} %get-tuple-element.63.n2_ref, bf16[1152,512]{1,0:T(8,128)(2,1)S(1)} %get-tuple-element.64.cot_ref, ...), custom_call_target="tpu_custom_call", output_to_operand_aliasing={{0}: (5, {}), {1}: (6, {})} | custom-call | flops 8000000000 | bytes 10485760 | tf_op jit(solution)/shard_map/mlp_first/pallas_call | solution.py:634
  48.8 7.3 %mlp_second.1 = (f32[1152,512]{1,0:T(8,128)}, f32[1152,512]{1,0:T(8,128)}, bf16[2048,512]{1,0:T(8,128)(2,1)}) custom-call(s32[1]{0:T(128)} %bitcast.3.me_ref.half_ref, bf16[1152,512]{1,0:T(8,128)(2,1)S(1)} %get-tuple-element.63.n2_ref, bf16[1152,512]{1,0:T(8,128)(2,1)S(1)} %get-tuple-element.64.cot_ref, bf16[512,2048]{1,0:T(8,128)(2,1)S(1)} %copy-done.5, ...), custom_call_target="tpu_custom_call" | custom-call | flops 8000000000 | bytes 10485760 | tf_op jit(solution)/shard_map/mlp_second/pallas_call | solution.py:634
  56.1 12.0 %all-to-all-start.1 = ((bf16[64,32,512]{2,1,0:T(8,128)(2,1)}), bf16[64,32,512]{2,1,0:T(8,128)(2,1)}, u32[]{:S(2)}, u32[]{:S(2)}) async-start(bf16[64,32,512]{2,1,0:T(8,128)(2,1)} %bitcast.13), calls=%async_computation.1 | async-start | bytes 4194304 | tf_op jit(solution)/shard_map/all_to_all | solution.py:780
  68.1 21.6 %back.1 = (bf16[1152,512]{1,0:T(8,128)(2,1)}, bf16[1152,512]{1,0:T(8,128)(2,1)}, bf16[1152,1536]{1,0:T(8,128)(2,1)}, f32[1,512]{1,0:T(1,128)S(1)}, bf16[1152,512...) custom-call(bf16[1152,512]{1,0:T(8,128)(2,1)} %get-tuple-element.61., ...), custom_call_target="tpu_custom_call" | custom-call | flops 24999999488 | bytes 10485760 | tf_op jit(solution)/shard_map/back/pallas_call | solution.py:652
  89.7 1.6 send.1
  92.1 1.6 keep.1.keep_ref
  95.8 10.0 %all-to-all-start = ((bf16[64,64,128]{2,1,0:T(8,128)(2,1)}), bf16[64,64,128]{2,1,0:T(8,128)(2,1)S(1)}, u32[]{:S(2)}, u32[]{:S(2)}) async-start(bf16[64,64,128]{2,1,0:T(8,128)(2,1)} %add.5.after_ref), calls=%async_computation | async-start | bytes 2097152 | tf_op jit(solution)/shard_map/all_to_all | solution.py:780
  105.8 8.3 %tokens.1 = (bf16[24,24,2,512]{3,2,1,0:T(2,128)(2,1)}, bf16[24,24,2,512]{3,2,1,0:T(2,128)(2,1)}, bf16[2,21,6,2,512]{4,3,2,1,0:T(2,128)(2,1)S(1)}, bf16[2,3,18,2,...) custom-call(bf16[1152,1536]{1,0:T(8,128)(2,1)} %get-tuple-element.77.dqkv_hbm, ...), custom_call_target="tpu_custom_call" | custom-call | flops 6000000000 | bytes 10485760 | tf_op jit(solution)/shard_map/tokens/pallas_call | solution.py:688
  114.1 2.5 %share_mlp.1.tile_ref = bf16[128,128]{1,0:T(8,128)(2,1)} custom-call(bf16[64,32,512]{2,1,0:T(8,128)(2,1)} %all-to-all-done.1.sums_ref, bf16[64,64,128]{2,1,0:T(8,128)(2,1)} %add.5.after_ref), custom_call_target="tpu_custom_call" | custom-call | flops 1000000000 | bytes 4194304 | tf_op jit(solution)/shard_map/share_mlp/pallas_call | solution.py:724
  116.6 6.4 %all-to-all-done.parts_ref = bf16[64,64,128]{2,1,0:T(8,128)(2,1)S(1)} async-done(((bf16[64,64,128]{2,1,0:T(8,128)(2,1)}), bf16[64,64,128]{2,1,0:T(8,128)(2,1)S(1)}, u32[]{:S(2)}, u32[]{:S(2)}) %all-to-all-start) | async-done | bytes 1048608 | tf_op jit(solution)/shard_map/all_to_all | solution.py:780
  123.8 2.4 %share.1 = bf16[64,200,128]{2,1,0:T(8,128)(2,1)} custom-call(bf16[64,64,128]{2,1,0:T(8,128)(2,1)S(1)} %all-to-all-done.parts_ref, bf16[128,128]{1,0:T(8,128)(2,1)S(1)} %copy-done.3, f32[1,512]{1,0:T(1,128)S(1)} %get-tuple-element.94.dg1_ref, f32[1,512]{1,0:T(1,128)S(1)} %get-tuple-element.95.dg2_ref), custom_call_target="tpu_custom_call" | custom-call | flops 1000000000 | bytes 4194304 | tf_op jit(solution)/shard_map/share/pallas_call | solution.py:724
  126.2 45.0 %all_to_all.15.all_ref = bf16[64,200,128]{2,1,0:T(8,128)(2,1)S(1)} all-to-all(bf16[64,200,128]{2,1,0:T(8,128)(2,1)} %share.1), channel_id=1, replica_groups=mesh['x'=4,'zl'=2,'zh'=2,'y'=4,'c'=2] {'y','x','zh','zl'}, dimensions={0} | all-to-all | bytes 6553600 | tf_op jit(solution)/shard_map/all_to_all | solution.py:780
  171.2 3.4 %collective-permute-start.8 = (bf16[64,200,128]{2,1,0:T(8,128)(2,1)S(1)}, bf16[64,200,128]{2,1,0:T(8,128)(2,1)S(1)}, u32[]{:S(2)}, u32[]{:S(2)}) collective-permute-start(bf16[64,200,128]{2,1,0:T(8,128)(2,1)S(1)} %all_to_all.15.all_ref), channel_id=1, source_target_pairs={{0,1},{1,0},{2,3},{3,2},{4,5},{5,4},{6,7},{7,6},{8,9},{9,8},{10,11... | collective-permute-start | bytes 9830408 | tf_op jit(solution)/shard_map/ppermute | solution.py:776
  175.4 3.0 %unpack_mine.1 = (f32[512,2048]{1,0:T(8,128)}, f32[2048,512]{1,0:T(8,128)}, f32[512,1536]{1,0:T(8,128)}, f32[512,512]{1,0:T(8,128)}, f32[8,128]{1,0:T(8,128)S(1)}) custom-call(s32[1]{0:T(128)} %bitcast.3.me_ref.half_ref, bf16[64,200,128]{2,1,0:T(8,128)(2,1)S(1)} %all_to_all.15.all_ref, f32[8,128]{1,0:T(8,128)S(1)} %broadcast_in_dim.3.gains_in), custom_call_target="tpu_custom_call" | custom-call | flops 1000000000 | bytes 10485760 | tf_op jit(solution)/shard_map/unpack_mine/pallas_call | solution.py:740
  178.4 1.7 collective-permute-done.8.all_ref
  180.1 3.0 %unpack_theirs.1 = (f32[512,2048]{1,0:T(8,128)}, f32[2048,512]{1,0:T(8,128)}, f32[512,1536]{1,0:T(8,128)}, f32[512,512]{1,0:T(8,128)}, f32[8,128]{1,0:T(8,128)S(1)}) custom-call(s32[1]{0:T(128)S(6)} %sub.4.half_ref, ...), custom_call_target="tpu_custom_call", output_to_operand_aliasing={{0}: (3, {}), {1}: (4, {}), {2}: (5, {}), {3}: (6, {})} | custom-call | flops 1000000000 | bytes 10485760 | tf_op jit(solution)/shard_map/unpack_theirs/pallas_call | solution.py:740
  183.6 5.9 %collective-permute-done.7.corner_ref = bf16[2,3,6,2,512]{4,3,2,1,0:T(2,128)(2,1)S(1)} collective-permute-done((bf16[2,3,6,2,512]{4,3,2,1,0:T(2,128)(2,1)S(1)}, bf16[2,3,6,2,512]{4,3,2,1,0:T(2,128)(2,1)S(1)}, u32[]{:S(2)}, u32[]{:S(2)}) %collective-permute-start.7) | collective-permute-done | bytes 73760 | tf_op jit(solution)/shard_map/ppermute | solution.py:771
  190.5 2.1 %place.1 = (bf16[24,24,2,512]{3,2,1,0:T(2,128)(2,1)}, bf16[24,24,2,512]{3,2,1,0:T(2,128)(2,1)}) custom-call(bf16[24,24,2,512]{3,2,1,0:T(2,128)(2,1)} %get-tuple-element.85.out_in, bf16[24,24,2,512]{3,2,1,0:T(2,128)(2,1)} %get-tuple-element.86.grad_in, bf16[2,21,6,2,512]{4,3,2,1,0:T(2,128)(2,1)} %copy-done.10, ...), custom_call_target="tpu_custom_call", output_to_operand_aliasing={{0}: (0, {}), {1}: (1, {})} | custom-call | flops 1000000000 | bytes 2097152 | tf_op jit(solution)/shard_map/place/pallas_call | solution.py:568
  (42 shorter events, 9.6 us)
Async XLA Ops:
  0.6 15.4 %copy-start = (bf16[24,24,2,512]{3,2,1,0:T(2,128)(2,1)S(1)}, bf16[24,24,2,512]{3,2,1,0:T(2,128)(2,1)}, u32[]{:S(2)}) copy-start(bf16[24,24,2,512]{3,2,1,0:T(2,128)(2,1)} %tok_ref.3) | copy-start | bytes 3538948
  0.6 15.4 %copy-start.1 = (bf16[24,24,2,512]{3,2,1,0:T(2,128)(2,1)S(1)}, bf16[24,24,2,512]{3,2,1,0:T(2,128)(2,1)}, u32[]{:S(2)}) copy-start(bf16[24,24,2,512]{3,2,1,0:T(2,128)(2,1)} %cot_ref.3) | copy-start | bytes 3538948
  0.7 15.4 %copy-start.9 = (f32[512]{0:T(512)S(1)}, f32[512]{0:T(512)}, u32[]{:S(2)}) copy-start(f32[512]{0:T(512)} %param.10) | copy-start | bytes 6148
  0.7 15.4 %copy-start.8 = (f32[512]{0:T(512)S(1)}, f32[512]{0:T(512)}, u32[]{:S(2)}) copy-start(f32[512]{0:T(512)} %param.13) | copy-start | bytes 6148
  2.1 0.8 copy-start.7
  2.9 13.1 %collective-permute-start = (bf16[2,21,6,2,512]{4,3,2,1,0:T(2,128)(2,1)}, bf16[2,21,6,2,512]{4,3,2,1,0:T(2,128)(2,1)S(1)}, u32[]{:S(2)}, u32[]{:S(2)}) collective-permute-start(bf16[2,21,6,2,512]{4,3,2,1,0:T(2,128)(2,1)} %copy-done.7), channel_id=1, source_target_pairs={{0,15},{1,0},{2,1},{3,2},{4,3},{5,4},{6,5},{7,6},{8,7},{9,8},{10,9... | collective-permute-start | bytes 1548296 | tf_op jit(solution)/shard_map/ppermute | solution.py:771
  4.3 11.7 %collective-permute-start.1 = (bf16[2,3,18,2,512]{4,3,2,1,0:T(2,128)(2,1)S(1)}, bf16[2,3,18,2,512]{4,3,2,1,0:T(2,128)(2,1)S(1)}, u32[]{:S(2)}, u32[]{:S(2)}) collective-permute-start(bf16[2,3,18,2,512]{4,3,2,1,0:T(2,128)(2,1)S(1)} %get-tuple-element.59), channel_id=1, source_target_pairs={{0,112},{1,113},{2,114},{3,115},{4,116},{5,117},{6,118},{7,119},{8... | collective-permute-start | bytes 663560 | tf_op jit(solution)/shard_map/ppermute | solution.py:771
  8.2 7.8 %collective-permute-start.2 = (bf16[2,3,6,2,512]{4,3,2,1,0:T(2,128)(2,1)S(1)}, bf16[2,3,6,2,512]{4,3,2,1,0:T(2,128)(2,1)S(1)}, u32[]{:S(2)}, u32[]{:S(2)}) collective-permute-start(bf16[2,3,6,2,512]{4,3,2,1,0:T(2,128)(2,1)S(1)} %get-tuple-element.60), channel_id=1, source_target_pairs={{0,127},{1,112},{2,113},{3,114},{4,115},{5,116},{6,117},{7,118},{8... | collective-permute-start | bytes 221192 | tf_op jit(solution)/shard_map/ppermute | solution.py:771
  16.0 12.7 %copy-start.5 = (bf16[512,2048]{1,0:T(8,128)(2,1)S(1)}, bf16[512,2048]{1,0:T(8,128)(2,1)}, u32[]{:S(2)}) copy-start(bf16[512,2048]{1,0:T(8,128)(2,1)} %wup_ref.5) | copy-start | bytes 6291460
  16.0 12.7 %copy-start.6 = (bf16[2048,512]{1,0:T(8,128)(2,1)S(1)}, bf16[2048,512]{1,0:T(8,128)(2,1)}, u32[]{:S(2)}) copy-start(bf16[2048,512]{1,0:T(8,128)(2,1)} %wdown_ref.5) | copy-start | bytes 6291460
  39.5 9.3 %collective-permute-start.3 = (bf16[2048,512]{1,0:T(8,128)(2,1)S(1)}, bf16[2048,512]{1,0:T(8,128)(2,1)S(1)}, u32[]{:S(2)}, u32[]{:S(2)}) collective-permute-start(bf16[2048,512]{1,0:T(8,128)(2,1)S(1)} %get-tuple-element.70), channel_id=1, source_target_pairs={{0,1},{1,0},{2,3},{3,2},{4,5},{5,4},{6,7},{7,6},{8,9},{9,8},{10,11... | collective-permute-start | bytes 6291464 | tf_op jit(solution)/shard_map/ppermute | solution.py:776
  56.1 39.6 %all-to-all-start.1 = ((bf16[64,32,512]{2,1,0:T(8,128)(2,1)}), bf16[64,32,512]{2,1,0:T(8,128)(2,1)}, u32[]{:S(2)}, u32[]{:S(2)}) async-start(bf16[64,32,512]{2,1,0:T(8,128)(2,1)} %bitcast.13), calls=%async_computation.1 | async-start | bytes 4194304 | tf_op jit(solution)/shard_map/all_to_all | solution.py:780
  91.3 3.1 %collective-permute-start.4 = (bf16[64,64,128]{2,1,0:T(8,128)(2,1)S(1)}, bf16[64,64,128]{2,1,0:T(8,128)(2,1)S(1)}, u32[]{:S(2)}, u32[]{:S(2)}) collective-permute-start(bf16[64,64,128]{2,1,0:T(8,128)(2,1)S(1)} %send.1), channel_id=1, source_target_pairs={{0,1},{1,0},{2,3},{3,2},{4,5},{5,4},{6,7},{7,6},{8,9},{9,8},{10,11... | collective-permute-start | bytes 3145736 | tf_op jit(solution)/shard_map/ppermute | solution.py:776
  95.6 10.2 %copy-start.2 = (bf16[64,64,128]{2,1,0:T(8,128)(2,1)S(1)}, bf16[64,64,128]{2,1,0:T(8,128)(2,1)}, u32[]{:S(2)}) copy-start(bf16[64,64,128]{2,1,0:T(8,128)(2,1)} %add.5.after_ref) | copy-start | bytes 3145732
  95.8 27.2 %all-to-all-start = ((bf16[64,64,128]{2,1,0:T(8,128)(2,1)}), bf16[64,64,128]{2,1,0:T(8,128)(2,1)S(1)}, u32[]{:S(2)}, u32[]{:S(2)}) async-start(bf16[64,64,128]{2,1,0:T(8,128)(2,1)} %add.5.after_ref), calls=%async_computation | async-start | bytes 2097152 | tf_op jit(solution)/shard_map/all_to_all | solution.py:780
  123.0 0.8 copy-start.3
  171.2 8.9 %collective-permute-start.8 = (bf16[64,200,128]{2,1,0:T(8,128)(2,1)S(1)}, bf16[64,200,128]{2,1,0:T(8,128)(2,1)S(1)}, u32[]{:S(2)}, u32[]{:S(2)}) collective-permute-start(bf16[64,200,128]{2,1,0:T(8,128)(2,1)S(1)} %all_to_all.15.all_ref), channel_id=1, source_target_pairs={{0,1},{1,0},{2,3},{3,2},{4,5},{5,4},{6,7},{7,6},{8,9},{9,8},{10,11... | collective-permute-start | bytes 9830408 | tf_op jit(solution)/shard_map/ppermute | solution.py:776
  174.6 15.0 %collective-permute-start.5 = (bf16[2,21,6,2,512]{4,3,2,1,0:T(2,128)(2,1)S(1)}, bf16[2,21,6,2,512]{4,3,2,1,0:T(2,128)(2,1)S(1)}, u32[]{:S(2)}, u32[]{:S(2)}) collective-permute-start(bf16[2,21,6,2,512]{4,3,2,1,0:T(2,128)(2,1)S(1)} %get-tuple-element.87), channel_id=1, source_target_pairs={{0,1},{1,2},{2,3},{3,4},{4,5},{5,6},{6,7},{7,8},{8,9},{9,10},{10,1... | collective-permute-start | bytes 1548296 | tf_op jit(solution)/shard_map/ppermute | solution.py:771
  174.6 15.0 %collective-permute-start.6 = (bf16[2,3,18,2,512]{4,3,2,1,0:T(2,128)(2,1)S(1)}, bf16[2,3,18,2,512]{4,3,2,1,0:T(2,128)(2,1)S(1)}, u32[]{:S(2)}, u32[]{:S(2)}) collective-permute-start(bf16[2,3,18,2,512]{4,3,2,1,0:T(2,128)(2,1)S(1)} %get-tuple-element.88), channel_id=1, source_target_pairs={{0,16},{1,17},{2,18},{3,19},{4,20},{5,21},{6,22},{7,23},{8,24},{9,... | collective-permute-start | bytes 663560 | tf_op jit(solution)/shard_map/ppermute | solution.py:771
  175.1 14.5 %collective-permute-start.7 = (bf16[2,3,6,2,512]{4,3,2,1,0:T(2,128)(2,1)S(1)}, bf16[2,3,6,2,512]{4,3,2,1,0:T(2,128)(2,1)S(1)}, u32[]{:S(2)}, u32[]{:S(2)}) collective-permute-start(bf16[2,3,6,2,512]{4,3,2,1,0:T(2,128)(2,1)S(1)} %get-tuple-element.89), channel_id=1, source_target_pairs={{0,17},{1,18},{2,19},{3,20},{4,21},{5,22},{6,23},{7,24},{8,25},{9,... | collective-permute-start | bytes 221192 | tf_op jit(solution)/shard_map/ppermute | solution.py:771
  183.0 6.6 %copy-start.4 = (f32[8,128]{1,0:T(8,128)}, f32[8,128]{1,0:T(8,128)S(1)}, u32[]{:S(2)}) copy-start(f32[8,128]{1,0:T(8,128)S(1)} %get-tuple-element.101.after_ref) | copy-start | bytes 12292
  189.6 0.6 copy-start.12
  189.6 0.7 copy-start.11
  189.6 0.9 copy-start.10
where the time goes:
time: 193 us
  Pallas kernels  85.1 us (44%)
  blocking collectives  45 us (23%)
  starting transfers between devices  41.6 us (22%)
  waiting for transfers between devices  16.9 us (9%)
  local copies, waits for them, and re-layouts  3.05 us (2%)
    all_to_all x1, blocking collectives, exchange(): return lax.all_to_all(parts, CHIPS, 0, 0, tiled=True)  45 us
    pallas_call x3, Pallas kernels, mlp(): pl.pallas_call(kernel, name='mlp_' + kind, in_specs=[SM, VM, VM, VM, VM]...  23.8 us
    all_to_all x2, starting transfers between devices, exchange(): return lax.all_to_all(parts, CHIPS, 0, 0, tiled=True)  22 us
    pallas_call x1, Pallas kernels, back(): pl.pallas_call(back_kernel, name='back', in_specs=[HB] * 9 + [VM], out_sp...  21.6 us
    pallas_call x1, Pallas kernels, front(): pl.pallas_call(front_kernel, name='front', in_specs=[SM] + [ANY] * 5 + [V...  12.7 us
    ppermute x6, starting transfers between devices, send_rims(): moved.append(lax.ppermute(block, LAT + LON, route))  11.9 us
    pallas_call x1, Pallas kernels, token_grads(): pl.pallas_call(tokens_kernel, name='tokens', in_specs=[HB] * 5 + [VM, ANY...  8.33 us
    ppermute x6, waiting for transfers between devices, send_rims(): moved.append(lax.ppermute(block, LAT + LON, route))  7.96 us
  transfers between devices with their start and end apart: 11, of which 6 were waited for; matrix products, arithmetic and copies ran while one was open for 0% of the time, Pallas kernels for 24%

commit v1 on v0

--- a/solution.py
+++ b/solution.py
@@ -148,7 +148,7 @@
 
     wqkv_copy.wait()
 
-    big = ROWS
+    big = tokens
 
     @pl.loop(0, tokens // big)
     def _(b):

time: 193 us -> 193 us (level)
  transfers between devices with their start and end apart: 11 -> 11, of which waited for: 6 -> 5; matrix products, arithmetic and copies ran while one was open for 0% -> 0% of each run, Pallas kernels for 24% -> 24%
where the time goes in v1:
time: 193 us; the launch traced here: 192 us
  Pallas kernels  84.8 us (44%)
  blocking collectives  45 us (23%)
  starting transfers between devices  41.8 us (22%)
  waiting for transfers between devices  16.7 us (9%)
  local copies, waits for them, and re-layouts  3.05 us (2%)
    all_to_all x1, blocking collectives, exchange(): return lax.all_to_all(parts, CHIPS, 0, 0, tiled=True)  45 us
    pallas_call x3, Pallas kernels, mlp(): pl.pallas_call(kernel, name='mlp_' + kind, in_specs=[SM, VM, VM, VM, VM]...  23.7 us
    all_to_all x2, starting transfers between devices, exchange(): return lax.all_to_all(parts, CHIPS, 0, 0, tiled=True)  22.1 us
    pallas_call x1, Pallas kernels, back(): pl.pallas_call(back_kernel, name='back', in_specs=[HB] * 9 + [VM], out_sp...  21.6 us
    pallas_call x1, Pallas kernels, front(): pl.pallas_call(front_kernel, name='front', in_specs=[SM] + [ANY] * 5 + [V...  12.3 us
    ppermute x6, starting transfers between devices, send_rims(): moved.append(lax.ppermute(block, LAT + LON, route))  11.9 us
    pallas_call x1, Pallas kernels, token_grads(): pl.pallas_call(tokens_kernel, name='tokens', in_specs=[HB] * 5 + [VM, ANY...  8.33 us
    ppermute x6, waiting for transfers between devices, send_rims(): moved.append(lax.ppermute(block, LAT + LON, route))  7.96 us
  transfers between devices with their start and end apart: 11, of which 5 were waited for; matrix products, arithmetic and copies ran while one was open for 0% of the time, Pallas kernels for 24%

profile of v1, /device:TPU:1, one launch (start us, length us, event | category | flops | bytes accessed | tf_op | source)
XLA Modules:
  0.0 192.5 jit_solution(4465626790073672509)
XLA Ops:
  4.3 3.9 %collective-permute-start.1 = (bf16[2,3,18,2,512]{4,3,2,1,0:T(2,128)(2,1)S(1)}, bf16[2,3,18,2,512]{4,3,2,1,0:T(2,128)(2,1)S(1)}, u32[]{:S(2)}, u32[]{:S(2)}) collective-permute-start(bf16[2,3,18,2,512]{4,3,2,1,0:T(2,128)(2,1)S(1)} %get-tuple-element.59), channel_id=1, source_target_pairs={{0,112},{1,113},{2,114},{3,115},{4,116},{5,117},{6,118},{7,119},{8... | collective-permute-start | bytes 663560 | tf_op jit(solution)/shard_map/ppermute | solution.py:771
  8.2 5.8 %collective-permute-start.2 = (bf16[2,3,6,2,512]{4,3,2,1,0:T(2,128)(2,1)S(1)}, bf16[2,3,6,2,512]{4,3,2,1,0:T(2,128)(2,1)S(1)}, u32[]{:S(2)}, u32[]{:S(2)}) collective-permute-start(bf16[2,3,6,2,512]{4,3,2,1,0:T(2,128)(2,1)S(1)} %get-tuple-element.60), channel_id=1, source_target_pairs={{0,127},{1,112},{2,113},{3,114},{4,115},{5,116},{6,117},{7,118},{8... | collective-permute-start | bytes 221192 | tf_op jit(solution)/shard_map/ppermute | solution.py:771
  14.0 2.0 %collective-permute-done.2.corner_ref = bf16[2,3,6,2,512]{4,3,2,1,0:T(2,128)(2,1)S(1)} collective-permute-done((bf16[2,3,6,2,512]{4,3,2,1,0:T(2,128)(2,1)S(1)}, bf16[2,3,6,2,512]{4,3,2,1,0:T(2,128)(2,1)S(1)}, u32[]{:S(2)}, u32[]{:S(2)}) %collective-permute-start.2) | collective-permute-done | bytes 73760 | tf_op jit(solution)/shard_map/ppermute | solution.py:771
  16.1 12.3 %front.1 = (bf16[1152,512]{1,0:T(8,128)(2,1)}, bf16[1152,512]{1,0:T(8,128)(2,1)}, bf16[1152,1536]{1,0:T(8,128)(2,1)}, bf16[8,8,144,144]{3,2,1,0:T(8,128)(2,1)}, ...) custom-call(s32[1]{0:T(128)} %bitcast.flag_ref, ...), custom_call_target="tpu_custom_call" | custom-call | flops 15000000512 | bytes 10485760 | tf_op jit(solution)/shard_map/front/pallas_call | solution.py:599
  28.4 10.7 %mlp_send.1 = (f32[1152,512]{1,0:T(8,128)S(1)}, f32[1152,512]{1,0:T(8,128)S(1)}, bf16[2048,512]{1,0:T(8,128)(2,1)S(1)}) custom-call(s32[1]{0:T(128)} %bitcast.3.me_ref.half_ref, bf16[1152,512]{1,0:T(8,128)(2,1)S(1)} %get-tuple-element.63.n2_ref, bf16[1152,512]{1,0:T(8,128)(2,1)S(1)} %get-tuple-element.64.cot_ref, bf16[512,2048]{1,0:T(8,128)(2,1)S(1)} %copy-done.5, ...), custom_call_target="tpu_custom_call" | custom-call | flops 16000000000 | bytes 10485760 | tf_op jit(solution)/shard_map/mlp_send/pallas_call | solution.py:634
  39.2 3.6 %collective-permute-start.3 = (bf16[2048,512]{1,0:T(8,128)(2,1)S(1)}, bf16[2048,512]{1,0:T(8,128)(2,1)S(1)}, u32[]{:S(2)}, u32[]{:S(2)}) collective-permute-start(bf16[2048,512]{1,0:T(8,128)(2,1)S(1)} %get-tuple-element.70), channel_id=1, source_target_pairs={{0,1},{1,0},{2,3},{3,2},{4,5},{5,4},{6,7},{7,6},{8,9},{9,8},{10,11... | collective-permute-start | bytes 6291464 | tf_op jit(solution)/shard_map/ppermute | solution.py:776
  42.7 5.7 %mlp_first.1 = (f32[1152,512]{1,0:T(8,128)S(1)}, f32[1152,512]{1,0:T(8,128)S(1)}, bf16[1024,512]{1,0:T(8,128)(2,1)S(1)}) custom-call(s32[1]{0:T(128)} %bitcast.3.me_ref.half_ref, bf16[1152,512]{1,0:T(8,128)(2,1)S(1)} %get-tuple-element.63.n2_ref, bf16[1152,512]{1,0:T(8,128)(2,1)S(1)} %get-tuple-element.64.cot_ref, ...), custom_call_target="tpu_custom_call", output_to_operand_aliasing={{0}: (5, {}), {1}: (6, {})} | custom-call | flops 8000000000 | bytes 10485760 | tf_op jit(solution)/shard_map/mlp_first/pallas_call | solution.py:634
  48.5 7.3 %mlp_second.1 = (f32[1152,512]{1,0:T(8,128)}, f32[1152,512]{1,0:T(8,128)}, bf16[2048,512]{1,0:T(8,128)(2,1)}) custom-call(s32[1]{0:T(128)} %bitcast.3.me_ref.half_ref, bf16[1152,512]{1,0:T(8,128)(2,1)S(1)} %get-tuple-element.63.n2_ref, bf16[1152,512]{1,0:T(8,128)(2,1)S(1)} %get-tuple-element.64.cot_ref, bf16[512,2048]{1,0:T(8,128)(2,1)S(1)} %copy-done.5, ...), custom_call_target="tpu_custom_call" | custom-call | flops 8000000000 | bytes 10485760 | tf_op jit(solution)/shard_map/mlp_second/pallas_call | solution.py:634
  55.8 12.0 %all-to-all-start.1 = ((bf16[64,32,512]{2,1,0:T(8,128)(2,1)}), bf16[64,32,512]{2,1,0:T(8,128)(2,1)}, u32[]{:S(2)}, u32[]{:S(2)}) async-start(bf16[64,32,512]{2,1,0:T(8,128)(2,1)} %bitcast.13), calls=%async_computation.1 | async-start | bytes 4194304 | tf_op jit(solution)/shard_map/all_to_all | solution.py:780
  67.7 21.6 %back.1 = (bf16[1152,512]{1,0:T(8,128)(2,1)}, bf16[1152,512]{1,0:T(8,128)(2,1)}, bf16[1152,1536]{1,0:T(8,128)(2,1)}, f32[1,512]{1,0:T(1,128)S(1)}, bf16[1152,512...) custom-call(bf16[1152,512]{1,0:T(8,128)(2,1)} %get-tuple-element.61., ...), custom_call_target="tpu_custom_call" | custom-call | flops 24999999488 | bytes 10485760 | tf_op jit(solution)/shard_map/back/pallas_call | solution.py:652
  89.3 1.6 send.1
  91.8 1.6 keep.1.keep_ref
  95.3 10.2 %all-to-all-start = ((bf16[64,64,128]{2,1,0:T(8,128)(2,1)}), bf16[64,64,128]{2,1,0:T(8,128)(2,1)S(1)}, u32[]{:S(2)}, u32[]{:S(2)}) async-start(bf16[64,64,128]{2,1,0:T(8,128)(2,1)} %add.5.after_ref), calls=%async_computation | async-start | bytes 2097152 | tf_op jit(solution)/shard_map/all_to_all | solution.py:780
  105.5 8.3 %tokens.1 = (bf16[24,24,2,512]{3,2,1,0:T(2,128)(2,1)}, bf16[24,24,2,512]{3,2,1,0:T(2,128)(2,1)}, bf16[2,21,6,2,512]{4,3,2,1,0:T(2,128)(2,1)S(1)}, bf16[2,3,18,2,...) custom-call(bf16[1152,1536]{1,0:T(8,128)(2,1)} %get-tuple-element.77.dqkv_hbm, ...), custom_call_target="tpu_custom_call" | custom-call | flops 6000000000 | bytes 10485760 | tf_op jit(solution)/shard_map/tokens/pallas_call | solution.py:688
  113.8 2.5 %share_mlp.1.tile_ref = bf16[128,128]{1,0:T(8,128)(2,1)} custom-call(bf16[64,32,512]{2,1,0:T(8,128)(2,1)} %all-to-all-done.1.sums_ref, bf16[64,64,128]{2,1,0:T(8,128)(2,1)} %add.5.after_ref), custom_call_target="tpu_custom_call" | custom-call | flops 1000000000 | bytes 4194304 | tf_op jit(solution)/shard_map/share_mlp/pallas_call | solution.py:724
  116.3 6.4 %all-to-all-done.parts_ref = bf16[64,64,128]{2,1,0:T(8,128)(2,1)S(1)} async-done(((bf16[64,64,128]{2,1,0:T(8,128)(2,1)}), bf16[64,64,128]{2,1,0:T(8,128)(2,1)S(1)}, u32[]{:S(2)}, u32[]{:S(2)}) %all-to-all-start) | async-done | bytes 1048608 | tf_op jit(solution)/shard_map/all_to_all | solution.py:780
  123.5 2.4 %share.1 = bf16[64,200,128]{2,1,0:T(8,128)(2,1)} custom-call(bf16[64,64,128]{2,1,0:T(8,128)(2,1)S(1)} %all-to-all-done.parts_ref, bf16[128,128]{1,0:T(8,128)(2,1)S(1)} %copy-done.3, f32[1,512]{1,0:T(1,128)S(1)} %get-tuple-element.94.dg1_ref, f32[1,512]{1,0:T(1,128)S(1)} %get-tuple-element.95.dg2_ref), custom_call_target="tpu_custom_call" | custom-call | flops 1000000000 | bytes 4194304 | tf_op jit(solution)/shard_map/share/pallas_call | solution.py:724
  125.9 45.0 %all_to_all.15.all_ref = bf16[64,200,128]{2,1,0:T(8,128)(2,1)S(1)} all-to-all(bf16[64,200,128]{2,1,0:T(8,128)(2,1)} %share.1), channel_id=1, replica_groups=mesh['x'=4,'zl'=2,'zh'=2,'y'=4,'c'=2] {'y','x','zh','zl'}, dimensions={0} | all-to-all | bytes 6553600 | tf_op jit(solution)/shard_map/all_to_all | solution.py:780
  170.9 3.4 %collective-permute-start.8 = (bf16[64,200,128]{2,1,0:T(8,128)(2,1)S(1)}, bf16[64,200,128]{2,1,0:T(8,128)(2,1)S(1)}, u32[]{:S(2)}, u32[]{:S(2)}) collective-permute-start(bf16[64,200,128]{2,1,0:T(8,128)(2,1)S(1)} %all_to_all.15.all_ref), channel_id=1, source_target_pairs={{0,1},{1,0},{2,3},{3,2},{4,5},{5,4},{6,7},{7,6},{8,9},{9,8},{10,11... | collective-permute-start | bytes 9830408 | tf_op jit(solution)/shard_map/ppermute | solution.py:776
  175.1 3.0 %unpack_mine.1 = (f32[512,2048]{1,0:T(8,128)}, f32[2048,512]{1,0:T(8,128)}, f32[512,1536]{1,0:T(8,128)}, f32[512,512]{1,0:T(8,128)}, f32[8,128]{1,0:T(8,128)S(1)}) custom-call(s32[1]{0:T(128)} %bitcast.3.me_ref.half_ref, bf16[64,200,128]{2,1,0:T(8,128)(2,1)S(1)} %all_to_all.15.all_ref, f32[8,128]{1,0:T(8,128)S(1)} %broadcast_in_dim.3.gains_in), custom_call_target="tpu_custom_call" | custom-call | flops 1000000000 | bytes 10485760 | tf_op jit(solution)/shard_map/unpack_mine/pallas_call | solution.py:740
  178.1 1.7 collective-permute-done.8.all_ref
  179.8 3.0 %unpack_theirs.1 = (f32[512,2048]{1,0:T(8,128)}, f32[2048,512]{1,0:T(8,128)}, f32[512,1536]{1,0:T(8,128)}, f32[512,512]{1,0:T(8,128)}, f32[8,128]{1,0:T(8,128)S(1)}) custom-call(s32[1]{0:T(128)S(6)} %sub.4.half_ref, ...), custom_call_target="tpu_custom_call", output_to_operand_aliasing={{0}: (3, {}), {1}: (4, {}), {2}: (5, {}), {3}: (6, {})} | custom-call | flops 1000000000 | bytes 10485760 | tf_op jit(solution)/shard_map/unpack_theirs/pallas_call | solution.py:740
  183.3 5.9 %collective-permute-done.7.corner_ref = bf16[2,3,6,2,512]{4,3,2,1,0:T(2,128)(2,1)S(1)} collective-permute-done((bf16[2,3,6,2,512]{4,3,2,1,0:T(2,128)(2,1)S(1)}, bf16[2,3,6,2,512]{4,3,2,1,0:T(2,128)(2,1)S(1)}, u32[]{:S(2)}, u32[]{:S(2)}) %collective-permute-start.7) | collective-permute-done | bytes 73760 | tf_op jit(solution)/shard_map/ppermute | solution.py:771
  190.2 2.1 %place.1 = (bf16[24,24,2,512]{3,2,1,0:T(2,128)(2,1)}, bf16[24,24,2,512]{3,2,1,0:T(2,128)(2,1)}) custom-call(bf16[24,24,2,512]{3,2,1,0:T(2,128)(2,1)} %get-tuple-element.85.out_in, bf16[24,24,2,512]{3,2,1,0:T(2,128)(2,1)} %get-tuple-element.86.grad_in, bf16[2,21,6,2,512]{4,3,2,1,0:T(2,128)(2,1)} %copy-done.10, ...), custom_call_target="tpu_custom_call", output_to_operand_aliasing={{0}: (0, {}), {1}: (1, {})} | custom-call | flops 1000000000 | bytes 2097152 | tf_op jit(solution)/shard_map/place/pallas_call | solution.py:568
  (42 shorter events, 9.5 us)
Async XLA Ops:
  0.6 15.4 %copy-start = (bf16[24,24,2,512]{3,2,1,0:T(2,128)(2,1)S(1)}, bf16[24,24,2,512]{3,2,1,0:T(2,128)(2,1)}, u32[]{:S(2)}) copy-start(bf16[24,24,2,512]{3,2,1,0:T(2,128)(2,1)} %tok_ref.3) | copy-start | bytes 3538948
  0.6 15.4 %copy-start.1 = (bf16[24,24,2,512]{3,2,1,0:T(2,128)(2,1)S(1)}, bf16[24,24,2,512]{3,2,1,0:T(2,128)(2,1)}, u32[]{:S(2)}) copy-start(bf16[24,24,2,512]{3,2,1,0:T(2,128)(2,1)} %cot_ref.3) | copy-start | bytes 3538948
  0.7 15.4 %copy-start.9 = (f32[512]{0:T(512)S(1)}, f32[512]{0:T(512)}, u32[]{:S(2)}) copy-start(f32[512]{0:T(512)} %param.10) | copy-start | bytes 6148
  0.7 15.4 %copy-start.8 = (f32[512]{0:T(512)S(1)}, f32[512]{0:T(512)}, u32[]{:S(2)}) copy-start(f32[512]{0:T(512)} %param.13) | copy-start | bytes 6148
  2.1 0.8 copy-start.7
  2.9 13.1 %collective-permute-start = (bf16[2,21,6,2,512]{4,3,2,1,0:T(2,128)(2,1)}, bf16[2,21,6,2,512]{4,3,2,1,0:T(2,128)(2,1)S(1)}, u32[]{:S(2)}, u32[]{:S(2)}) collective-permute-start(bf16[2,21,6,2,512]{4,3,2,1,0:T(2,128)(2,1)} %copy-done.7), channel_id=1, source_target_pairs={{0,15},{1,0},{2,1},{3,2},{4,3},{5,4},{6,5},{7,6},{8,7},{9,8},{10,9... | collective-permute-start | bytes 1548296 | tf_op jit(solution)/shard_map/ppermute | solution.py:771
  4.3 11.7 %collective-permute-start.1 = (bf16[2,3,18,2,512]{4,3,2,1,0:T(2,128)(2,1)S(1)}, bf16[2,3,18,2,512]{4,3,2,1,0:T(2,128)(2,1)S(1)}, u32[]{:S(2)}, u32[]{:S(2)}) collective-permute-start(bf16[2,3,18,2,512]{4,3,2,1,0:T(2,128)(2,1)S(1)} %get-tuple-element.59), channel_id=1, source_target_pairs={{0,112},{1,113},{2,114},{3,115},{4,116},{5,117},{6,118},{7,119},{8... | collective-permute-start | bytes 663560 | tf_op jit(solution)/shard_map/ppermute | solution.py:771
  8.2 7.8 %collective-permute-start.2 = (bf16[2,3,6,2,512]{4,3,2,1,0:T(2,128)(2,1)S(1)}, bf16[2,3,6,2,512]{4,3,2,1,0:T(2,128)(2,1)S(1)}, u32[]{:S(2)}, u32[]{:S(2)}) collective-permute-start(bf16[2,3,6,2,512]{4,3,2,1,0:T(2,128)(2,1)S(1)} %get-tuple-element.60), channel_id=1, source_target_pairs={{0,127},{1,112},{2,113},{3,114},{4,115},{5,116},{6,117},{7,118},{8... | collective-permute-start | bytes 221192 | tf_op jit(solution)/shard_map/ppermute | solution.py:771
  16.0 12.4 %copy-start.5 = (bf16[512,2048]{1,0:T(8,128)(2,1)S(1)}, bf16[512,2048]{1,0:T(8,128)(2,1)}, u32[]{:S(2)}) copy-start(bf16[512,2048]{1,0:T(8,128)(2,1)} %wup_ref.5) | copy-start | bytes 6291460
  16.0 12.4 %copy-start.6 = (bf16[2048,512]{1,0:T(8,128)(2,1)S(1)}, bf16[2048,512]{1,0:T(8,128)(2,1)}, u32[]{:S(2)}) copy-start(bf16[2048,512]{1,0:T(8,128)(2,1)} %wdown_ref.5) | copy-start | bytes 6291460
  39.2 9.3 %collective-permute-start.3 = (bf16[2048,512]{1,0:T(8,128)(2,1)S(1)}, bf16[2048,512]{1,0:T(8,128)(2,1)S(1)}, u32[]{:S(2)}, u32[]{:S(2)}) collective-permute-start(bf16[2048,512]{1,0:T(8,128)(2,1)S(1)} %get-tuple-element.70), channel_id=1, source_target_pairs={{0,1},{1,0},{2,3},{3,2},{4,5},{5,4},{6,7},{7,6},{8,9},{9,8},{10,11... | collective-permute-start | bytes 6291464 | tf_op jit(solution)/shard_map/ppermute | solution.py:776
  55.8 39.5 %all-to-all-start.1 = ((bf16[64,32,512]{2,1,0:T(8,128)(2,1)}), bf16[64,32,512]{2,1,0:T(8,128)(2,1)}, u32[]{:S(2)}, u32[]{:S(2)}) async-start(bf16[64,32,512]{2,1,0:T(8,128)(2,1)} %bitcast.13), calls=%async_computation.1 | async-start | bytes 4194304 | tf_op jit(solution)/shard_map/all_to_all | solution.py:780
  90.9 3.2 %collective-permute-start.4 = (bf16[64,64,128]{2,1,0:T(8,128)(2,1)S(1)}, bf16[64,64,128]{2,1,0:T(8,128)(2,1)S(1)}, u32[]{:S(2)}, u32[]{:S(2)}) collective-permute-start(bf16[64,64,128]{2,1,0:T(8,128)(2,1)S(1)} %send.1), channel_id=1, source_target_pairs={{0,1},{1,0},{2,3},{3,2},{4,5},{5,4},{6,7},{7,6},{8,9},{9,8},{10,11... | collective-permute-start | bytes 3145736 | tf_op jit(solution)/shard_map/ppermute | solution.py:776
  95.3 10.2 %copy-start.2 = (bf16[64,64,128]{2,1,0:T(8,128)(2,1)S(1)}, bf16[64,64,128]{2,1,0:T(8,128)(2,1)}, u32[]{:S(2)}) copy-start(bf16[64,64,128]{2,1,0:T(8,128)(2,1)} %add.5.after_ref) | copy-start | bytes 3145732
  95.3 27.4 %all-to-all-start = ((bf16[64,64,128]{2,1,0:T(8,128)(2,1)}), bf16[64,64,128]{2,1,0:T(8,128)(2,1)S(1)}, u32[]{:S(2)}, u32[]{:S(2)}) async-start(bf16[64,64,128]{2,1,0:T(8,128)(2,1)} %add.5.after_ref), calls=%async_computation | async-start | bytes 2097152 | tf_op jit(solution)/shard_map/all_to_all | solution.py:780
  122.7 0.8 copy-start.3
  170.9 8.9 %collective-permute-start.8 = (bf16[64,200,128]{2,1,0:T(8,128)(2,1)S(1)}, bf16[64,200,128]{2,1,0:T(8,128)(2,1)S(1)}, u32[]{:S(2)}, u32[]{:S(2)}) collective-permute-start(bf16[64,200,128]{2,1,0:T(8,128)(2,1)S(1)} %all_to_all.15.all_ref), channel_id=1, source_target_pairs={{0,1},{1,0},{2,3},{3,2},{4,5},{5,4},{6,7},{7,6},{8,9},{9,8},{10,11... | collective-permute-start | bytes 9830408 | tf_op jit(solution)/shard_map/ppermute | solution.py:776
  174.3 15.0 %collective-permute-start.5 = (bf16[2,21,6,2,512]{4,3,2,1,0:T(2,128)(2,1)S(1)}, bf16[2,21,6,2,512]{4,3,2,1,0:T(2,128)(2,1)S(1)}, u32[]{:S(2)}, u32[]{:S(2)}) collective-permute-start(bf16[2,21,6,2,512]{4,3,2,1,0:T(2,128)(2,1)S(1)} %get-tuple-element.87), channel_id=1, source_target_pairs={{0,1},{1,2},{2,3},{3,4},{4,5},{5,6},{6,7},{7,8},{8,9},{9,10},{10,1... | collective-permute-start | bytes 1548296 | tf_op jit(solution)/shard_map/ppermute | solution.py:771
  174.3 15.0 %collective-permute-start.6 = (bf16[2,3,18,2,512]{4,3,2,1,0:T(2,128)(2,1)S(1)}, bf16[2,3,18,2,512]{4,3,2,1,0:T(2,128)(2,1)S(1)}, u32[]{:S(2)}, u32[]{:S(2)}) collective-permute-start(bf16[2,3,18,2,512]{4,3,2,1,0:T(2,128)(2,1)S(1)} %get-tuple-element.88), channel_id=1, source_target_pairs={{0,16},{1,17},{2,18},{3,19},{4,20},{5,21},{6,22},{7,23},{8,24},{9,... | collective-permute-start | bytes 663560 | tf_op jit(solution)/shard_map/ppermute | solution.py:771
  174.8 14.5 %collective-permute-start.7 = (bf16[2,3,6,2,512]{4,3,2,1,0:T(2,128)(2,1)S(1)}, bf16[2,3,6,2,512]{4,3,2,1,0:T(2,128)(2,1)S(1)}, u32[]{:S(2)}, u32[]{:S(2)}) collective-permute-start(bf16[2,3,6,2,512]{4,3,2,1,0:T(2,128)(2,1)S(1)} %get-tuple-element.89), channel_id=1, source_target_pairs={{0,17},{1,18},{2,19},{3,20},{4,21},{5,22},{6,23},{7,24},{8,25},{9,... | collective-permute-start | bytes 221192 | tf_op jit(solution)/shard_map/ppermute | solution.py:771
  182.7 6.6 %copy-start.4 = (f32[8,128]{1,0:T(8,128)}, f32[8,128]{1,0:T(8,128)S(1)}, u32[]{:S(2)}) copy-start(f32[8,128]{1,0:T(8,128)S(1)} %get-tuple-element.101.after_ref) | copy-start | bytes 12292
  189.3 0.6 copy-start.12
  189.3 0.7 copy-start.11
  189.3 0.9 copy-start.10
